TPU v7x, 32 devices: a whole 2x2x4 slice. The times are simulated.
32 devices in a mesh: groups: 2 (over x), mp: 8 (over z, y), dp: 2 (over core).
Axes of the slice: x: 2, y: 2, z: 4, core: 2. Of those that a mesh axis runs over, the one named last changes fastest.
Arguments:
- latents: bfloat16 [12, 128, 128, 320], P(('groups', 'dp'), 'mp'), parts along dimension 0, may hold values from -6 to 6
- room_labels: int32 [12, 128, 128], P(('groups', 'dp'), 'mp'), parts along dimension 0, may hold values from 0 to 15
- timesteps: int32 [12], P(('groups', 'dp')), parts along dimension 0, may hold values from 0 to 999
- label_table: bfloat16 [16, 320], replicated, may hold values from -6 to 6
- time_weight: bfloat16 [1280, 320], replicated, may hold values from -0.15625 to 0.15625
- trunk_weight: bfloat16 [320, 3, 3, 320], P('mp'), may hold values from -0.109375 to 0.109375
- control_weight: bfloat16 [320, 3, 3, 320], P('mp'), may hold values from -0.109375 to 0.109375
- mix_weight: bfloat16 [320, 320], P('mp'), may hold values from -0.3125 to 0.3125
- cotangent: bfloat16 [12, 128, 128, 320], P(('groups', 'dp'), 'mp'), parts along dimension 0, may hold values from -0.08984375 to 0.08984375
Outputs:
- output: bfloat16 [12, 128, 128, 320], P(('groups', 'dp'), 'mp'), parts along dimension 0
- grad_control: float32 [640, 3, 3, 320], P(('groups', 'mp')), parts along dimension 0
- grad_mix: float32 [640, 320], P(('groups', 'mp')), parts along dimension 0
- grad_table: float32 [32, 320], P('groups'), parts along dimension 0
There are 2 independent parts, one for each index of `groups`. A program takes and returns all parts, laid end to end along the dimension named above; an argument that names none is the same for every part. Nothing has to cross between parts.
All inputs are finite; a program needn't handle non-finite values.
Results may differ from a plain program's by a relative error of at most 0.0057.
Values may be sent and summed in bfloat16 or wider, within the bound.
A program may use at most 256 MiB of HBM per device.

v0:
```python
import math
import jax
import jax.numpy as jnp
from jax import lax
from jax.sharding import PartitionSpec as P


def with_halo(cells, sides, width):
    for axis, dim in sides:
        count = lax.axis_size(axis)
        ends = count - 1
        head = lax.slice_in_dim(cells, 0, width, axis=dim)
        tail = lax.slice_in_dim(cells, cells.shape[dim] - width, cells.shape[dim], axis=dim)
        cells = jnp.concatenate(
            [
                lax.ppermute(tail, axis, [(i, (i + 1) % count) for i in range(ends)]),
                cells,
                lax.ppermute(head, axis, [((i + 1) % count, i) for i in range(ends)]),
            ],
            axis=dim,
        )
    return cells


def sinusoid(timesteps, embed_width):
    half_width = embed_width // 2
    indices = jnp.arange(half_width, dtype=jnp.float32)
    frequency = jnp.exp(-math.log(10000.0) * indices / half_width)
    angles = timesteps.astype(jnp.float32)[:, None] * frequency[None, :]
    return jnp.concatenate([jnp.cos(angles), jnp.sin(angles)], axis=1)


def forward_taps(frame, kernel):
    row_count = frame.shape[1] - 2
    span_cols = frame.shape[2] - 2
    running = jnp.zeros(frame.shape[:1] + (row_count, span_cols, kernel.shape[3]), jnp.float32)
    for tap_row in range(3):
        for tap_col in range(3):
            running = running + jnp.einsum(
                "bhwc,cd->bhwd",
                frame[:, tap_row : tap_row + row_count, tap_col : tap_col + span_cols],
                kernel[:, tap_row, tap_col],
                preferred_element_type=jnp.float32,
            )
    return running


def backward_taps(frame, kernel):
    row_count = frame.shape[1] - 2
    span_cols = frame.shape[2] - 2
    running = jnp.zeros(frame.shape[:1] + (row_count, span_cols, kernel.shape[0]), jnp.float32)
    for tap_row in range(3):
        for tap_col in range(3):
            running = running + jnp.einsum(
                "bhwd,cd->bhwc",
                frame[
                    :, 2 - tap_row : 2 - tap_row + row_count, 2 - tap_col : 2 - tap_col + span_cols
                ],
                kernel[:, tap_row, tap_col],
                preferred_element_type=jnp.float32,
            )
    return running


def per_device(
    latents,
    room_labels,
    timesteps,
    label_table,
    time_weight,
    trunk_weight,
    control_weight,
    mix_weight,
    cotangent,
):
    images, row_count, span_cols, channels = latents.shape
    rooms = label_table.shape[0]
    onehot = (room_labels[..., None] == jnp.arange(rooms, dtype=jnp.int32)).astype(jnp.bfloat16)
    embedded = jnp.einsum("bhwr,rc->bhwc", onehot, label_table, preferred_element_type=jnp.float32)
    control_in = (latents.astype(jnp.float32) + embedded).astype(jnp.bfloat16)
    stacked = jnp.stack([latents, control_in])
    framed = with_halo(stacked, (("mp", 2),), 1)
    framed = jnp.pad(framed, ((0, 0), (0, 0), (0, 0), (1, 1), (0, 0)))
    trunk_frame = framed[0]
    control_frame = framed[1]
    time_features = jax.nn.silu(sinusoid(timesteps, time_weight.shape[0])).astype(jnp.bfloat16)
    time_shift = jnp.dot(time_features, time_weight, preferred_element_type=jnp.float32)[
        :, None, None, :
    ]
    trunk_full = lax.all_gather(trunk_weight, "mp", axis=0, tiled=True)
    trunk_pre = forward_taps(trunk_frame, trunk_full) + time_shift
    control_full, mix_full = (
        lax.all_gather(control_weight, "mp", axis=0, tiled=True),
        lax.all_gather(mix_weight, "mp", axis=0, tiled=True),
    )
    control_pre = forward_taps(control_frame, control_full) + time_shift
    gated_act = jax.nn.silu(control_pre).astype(jnp.bfloat16)
    mixed_out = jnp.einsum("bhwc,cd->bhwd", gated_act, mix_full, preferred_element_type=jnp.float32)
    output = (jax.nn.silu(trunk_pre) + mixed_out).astype(jnp.bfloat16)
    back_gate = jnp.einsum("bhwd,cd->bhwc", cotangent, mix_full, preferred_element_type=jnp.float32)
    sigmoid_val = jax.nn.sigmoid(control_pre)
    back_pre = (back_gate * sigmoid_val * (1.0 + control_pre * (1.0 - sigmoid_val))).astype(
        jnp.bfloat16
    )
    back_frame = with_halo(back_pre, (("mp", 1),), 1)
    back_frame = jnp.pad(back_frame, ((0, 0), (0, 0), (1, 1), (0, 0)))
    back_kernel = lax.all_gather(control_weight, "mp", axis=0, tiled=True)
    back_in = backward_taps(back_frame, back_kernel)
    table_local = jnp.einsum(
        "bhwr,bhwc->rc", onehot.astype(jnp.float32), back_in, precision=lax.Precision.HIGHEST
    )
    grad_table = lax.psum(table_local, ("mp", "dp"))
    pieces = []
    for tap_row in range(3):
        for tap_col in range(3):
            pieces.append(
                jnp.einsum(
                    "bhwc,bhwd->cd",
                    control_frame[:, tap_row : tap_row + row_count, tap_col : tap_col + span_cols],
                    back_pre,
                    preferred_element_type=jnp.float32,
                )
            )
    kernel_rows = jnp.stack(pieces, axis=1).reshape(channels, 9 * channels)
    mix_rows = jnp.einsum("bhwc,bhwd->cd", gated_act, cotangent, preferred_element_type=jnp.float32)
    grad_term = jnp.concatenate([kernel_rows, mix_rows], axis=1)
    grad_rows = lax.psum_scatter(grad_term, "mp", scatter_dimension=0, tiled=True)
    grad_rows = lax.psum(grad_rows, "dp")
    grad_control = grad_rows[:, : 9 * channels].reshape(grad_rows.shape[0], 3, 3, channels)
    grad_mix = grad_rows[:, 9 * channels :]
    return (output, grad_control, grad_mix, grad_table)


def solution(mesh):
    in_specs = (
        P(("groups", "dp"), "mp", None, None),
        P(("groups", "dp"), "mp", None),
        P(("groups", "dp")),
        P(),
        P(),
        P("mp", None, None, None),
        P("mp", None, None, None),
        P("mp", None),
        P(("groups", "dp"), "mp", None, None),
    )
    out_specs = (
        P(("groups", "dp"), "mp", None, None),
        P(("groups", "mp"), None, None, None),
        P(("groups", "mp"), None),
        P("groups", None),
    )
    return jax.shard_map(
        per_device, mesh=mesh, in_specs=in_specs, out_specs=out_specs, check_vma=False
    )
```

profile of v0, /device:TPU:0, one launch (start us, length us, event | category | flops | bytes accessed | tf_op | source)
XLA Modules:
  0.0 456.9 jit_solution(16254729280796380880)
XLA Ops:
  8.0 3.5 fusion.27
  13.5 4.9 %collective-permute-start = (bf16[2,3,1,128,320]{3,4,2,1,0:T(8,128)(2,1)S(1)}, bf16[2,3,1,128,320]{3,4,2,1,0:T(8,128)(2,1)S(1)}, u32[]{:S(2)}, u32[]{:S(2)}) collective-permute-start(bf16[2,3,1,128,320]{3,4,2,1,0:T(8,128)(2,1)S(1)} %get-tuple-element.14), channel_id=1, source_target_pairs={{0,2},{2,4},{4,6},{6,8},{8,10},{10,12},{12,14},{1,3},{3,5},{5,7},{... | collective-permute-start | bytes 1474568 | tf_op jit(solution)/shard_map/ppermute | solution.py:16
  19.7 49.6 %all_gather.12 = bf16[320,320]{1,0:T(8,128)(2,1)S(1)} all-gather(bf16[40,320]{1,0:T(8,128)(2,1)S(1)} %copy-done.13), channel_id=1, replica_groups=mesh['groups'=2,'mp'=8,'dp'=2] {'mp'}, dimensions={0}, use_global_device_ids=true | all-gather | bytes 230400 | tf_op jit(solution)/shard_map/all_gather | solution.py:94
  69.9 18.2 %select_maximum_fusion = bf16[2,3,18,130,320]{3,4,2,1,0:T(8,128)(2,1)S(1)} fusion(bf16[2,3,1,128,320]{3,4,2,1,0:T(8,128)(2,1)S(1)} %collective-permute-done.1, bf16[2,3,1,128,320]{3,4,2,1,0:T(8,128)(2,1)S(1)} %collective-permute-done, bf16[1,3,16,128,320]{3,4,2,1,0:T(8,128)(2,1)} %copy-done.6, bf16[1,3,16,128,320]{3,4,2,1,0:T(8,128)(2,1)} %bitcast.302), kind=kLoop, calls=%fused_computation.5 | loop fusion | flops 67392000 | bytes 17832960 | tf_op jit(solution)/shard_map/concatenate | solution.py:14
  88.1 6.6 %slice_bitcast_fusion.1 = (bf16[3,18,130,320]{2,3,1,0:T(8,128)(2,1)}, bf16[3,18,130,320]{2,3,1,0:T(8,128)(2,1)}) fusion(bf16[2,3,18,130,320]{3,4,2,1,0:T(8,128)(2,1)S(1)} %select_maximum_fusion), kind=kLoop, calls=%fused_computation.17 | loop fusion | bytes 17971200 | tf_op jit(solution)/shard_map/squeeze | solution.py:84
  94.7 9.1 %fusion.64 = f32[3,16,128,320]{2,3,1,0:T(8,128)} fusion(bf16[3,18,130,320]{2,3,1,0:T(8,128)(2,1)} %get-tuple-element.13, bf16[320,3,3,320]{3,0,2,1:T(8,128)(2,1)} %all-gather.5.cloned.1.call-done), kind=kOutput, calls=%fused_computation.79 | convolution fusion | flops 1258291200 | bytes 12042240 | tf_op jit(solution)/shard_map/bhwc,cd->bhwd/dot_general | solution.py:39
  103.8 5.3 %fusion.68 = f32[3,16,128,320]{2,3,1,0:T(8,128)} fusion(bf16[3,18,130,320]{2,3,1,0:T(8,128)(2,1)S(1)} %copy-done.2, bf16[320,3,3,320]{3,0,2,1:T(8,128)(2,1)S(1)} %copy-done.9), kind=kOutput, calls=%fused_computation.83 | convolution fusion | flops 1258291200 | bytes 12042240 | tf_op jit(solution)/shard_map/bhwc,cd->bhwd/dot_general | solution.py:39
  109.1 5.5 %fusion.72 = f32[3,16,128,320]{2,3,1,0:T(8,128)} fusion(bf16[3,18,130,320]{2,3,1,0:T(8,128)(2,1)S(1)} %copy-done.2, bf16[320,3,3,320]{3,0,2,1:T(8,128)(2,1)S(1)} %copy-done.9), kind=kOutput, calls=%fused_computation.87 | convolution fusion | flops 1258291200 | bytes 12042240 | tf_op jit(solution)/shard_map/bhwc,cd->bhwd/dot_general | solution.py:39
  114.6 5.5 %fusion.76 = f32[3,16,128,320]{2,3,1,0:T(8,128)} fusion(bf16[3,18,130,320]{2,3,1,0:T(8,128)(2,1)S(1)} %copy-done.2, bf16[320,3,3,320]{3,0,2,1:T(8,128)(2,1)S(1)} %copy-done.9), kind=kOutput, calls=%fused_computation.91 | convolution fusion | flops 1258291200 | bytes 12042240 | tf_op jit(solution)/shard_map/bhwc,cd->bhwd/dot_general | solution.py:39
  120.2 5.3 %fusion.80 = f32[3,16,128,320]{2,3,1,0:T(8,128)} fusion(bf16[3,18,130,320]{2,3,1,0:T(8,128)(2,1)S(1)} %copy-done.2, bf16[320,3,3,320]{3,0,2,1:T(8,128)(2,1)S(1)} %copy-done.9), kind=kOutput, calls=%fused_computation.95 | convolution fusion | flops 1258291200 | bytes 12042240 | tf_op jit(solution)/shard_map/bhwc,cd->bhwd/dot_general | solution.py:39
  125.5 5.8 %fusion.84 = f32[3,16,128,320]{2,3,1,0:T(8,128)} fusion(bf16[3,18,130,320]{2,3,1,0:T(8,128)(2,1)S(1)} %copy-done.2, bf16[320,3,3,320]{3,0,2,1:T(8,128)(2,1)S(1)} %copy-done.9), kind=kOutput, calls=%fused_computation.99 | convolution fusion | flops 1258291200 | bytes 12042240 | tf_op jit(solution)/shard_map/bhwc,cd->bhwd/dot_general | solution.py:39
  131.3 5.7 %fusion.88 = f32[3,16,128,320]{2,3,1,0:T(8,128)} fusion(bf16[3,18,130,320]{2,3,1,0:T(8,128)(2,1)S(1)} %copy-done.2, bf16[320,3,3,320]{3,0,2,1:T(8,128)(2,1)S(1)} %copy-done.9), kind=kOutput, calls=%fused_computation.103 | convolution fusion | flops 1258291200 | bytes 12042240 | tf_op jit(solution)/shard_map/bhwc,cd->bhwd/dot_general | solution.py:39
  137.0 5.4 %fusion.92 = f32[3,16,128,320]{2,3,1,0:T(8,128)} fusion(bf16[3,18,130,320]{2,3,1,0:T(8,128)(2,1)S(1)} %copy-done.2, bf16[320,3,3,320]{3,0,2,1:T(8,128)(2,1)S(1)} %copy-done.9), kind=kOutput, calls=%fused_computation.107 | convolution fusion | flops 1258291200 | bytes 12042240 | tf_op jit(solution)/shard_map/bhwc,cd->bhwd/dot_general | solution.py:39
  142.4 28.2 %multiply_convert_fusion.1 = (bf16[3,16,128,320]{2,3,1,0:T(8,128)(2,1)}, f32[3,16,128,320]{2,3,1,0:T(8,128)}) fusion(f32[3,320]{1,0:T(4,128)S(1)} %fusion.163, bf16[3,18,130,320]{2,3,1,0:T(8,128)(2,1)} %get-tuple-element.13, bf16[320,3,3,320]{3,0,2,1:T(8,128)(2,1)S(1)} %copy-done.9, f32[3,16,128,320]{2,3,1,0:T(8,128)} %fusion.64, ...), kind=kOutput, calls=%fused_computation.29 | convolution fusion | flops 1285816320 | bytes 78895104 | tf_op jit(solution)/shard_map/bhwc,cd->bhwd/dot_general | solution.py:39
  170.6 7.3 %multiply_convert_fusion = bf16[3,16,128,320]{2,3,1,0:T(8,128)(2,1)S(1)} fusion(f32[3,16,128,320]{2,3,1,0:T(8,128)} %get-tuple-element.21, bf16[3,16,128,320]{2,3,1,0:T(8,128)(2,1)} %param.17, bf16[320,320]{1,0:T(8,128)(2,1)S(1)} %all_gather.12), kind=kOutput, calls=%fused_computation.27 | convolution fusion | flops 1275985920 | bytes 15933440 | tf_op jit(solution)/shard_map/bhwd,cd->bhwc/dot_general | solution.py:100
  178.0 5.7 %fusion.101 = f32[320,9,320]{0,2,1:T(8,128)S(1)} fusion(bf16[3,16,128,320]{2,3,1,0:T(8,128)(2,1)S(1)} %multiply_convert_fusion, bf16[3,18,130,320]{2,3,1,0:T(8,128)(2,1)} %get-tuple-element.13), kind=kOutput, calls=%fused_computation.110 | convolution fusion | flops 1258291200 | bytes 8355840 | tf_op jit(solution)/shard_map/bhwc,bhwd->cd/dot_general | solution.py:117
  187.0 5.5 %fusion.107 = f32[320,9,320]{0,2,1:T(8,128)S(1)} fusion(f32[320,9,320]{0,2,1:T(8,128)S(1)} %fusion.101, bf16[3,16,128,320]{2,3,1,0:T(8,128)(2,1)S(1)} %multiply_convert_fusion, bf16[3,18,130,320]{2,3,1,0:T(8,128)(2,1)} %get-tuple-element.13), kind=kOutput, calls=%fused_computation.112 | convolution fusion | flops 1258291200 | bytes 8355840 | tf_op jit(solution)/shard_map/bhwc,bhwd->cd/dot_general | solution.py:117
  192.5 2.3 fusion.113
  194.8 2.2 fusion.119
  197.0 2.3 fusion.125
  199.3 2.3 fusion.131
  201.6 2.2 fusion.137
  203.8 2.5 fusion.143
  206.3 2.3 fusion.149
  210.8 5.6 %copy.38 = f32[320,2880]{1,0:T(8,128)} copy(f32[320,2880]{0,1:T(8,128)} %bitcast.304) | data formatting | bytes 7372800 | tf_op jit(solution)/shard_map/reshape | solution.py:124
  216.4 7.6 %fusion.156 = f32[3,16,128,320]{2,3,1,0:T(8,128)} fusion(bf16[3,16,128,320]{2,3,1,0:T(8,128)(2,1)} %get-tuple-element.20, bf16[320,320]{1,0:T(8,128)(2,1)S(1)} %all_gather.12), kind=kOutput, calls=%fused_computation.151 | convolution fusion | flops 1258291200 | bytes 12001280 | tf_op jit(solution)/shard_map/bhwc,cd->bhwd/dot_general | solution.py:98
  226.2 2.3 pad_maximum_fusion
  228.7 9.0 %fusion.42 = f32[3,16,128,320]{2,3,1,0:T(8,128)} fusion(bf16[3,18,130,320]{2,3,1,0:T(8,128)(2,1)} %get-tuple-element.12, bf16[320,3,3,320]{3,0,2,1:T(8,128)(2,1)} %all-gather.3.cloned.1.call-done), kind=kOutput, calls=%fused_computation.57 | convolution fusion | flops 1258291200 | bytes 12042240 | tf_op jit(solution)/shard_map/bhwc,cd->bhwd/dot_general | solution.py:39
  237.7 7.5 %fusion.44 = f32[3,16,128,320]{2,3,1,0:T(8,128)} fusion(bf16[3,18,130,320]{2,3,1,0:T(8,128)(2,1)} %get-tuple-element.12, bf16[320,3,3,320]{3,0,2,1:T(8,128)(2,1)S(1)} %copy-done.11), kind=kOutput, calls=%fused_computation.59 | convolution fusion | flops 1258291200 | bytes 12042240 | tf_op jit(solution)/shard_map/bhwc,cd->bhwd/dot_general | solution.py:39
  245.2 5.5 %fusion.46 = f32[3,16,128,320]{2,3,1,0:T(8,128)} fusion(bf16[3,18,130,320]{2,3,1,0:T(8,128)(2,1)S(1)} %bitcast.299, bf16[320,3,3,320]{3,0,2,1:T(8,128)(2,1)S(1)} %copy-done.11), kind=kOutput, calls=%fused_computation.61 | convolution fusion | flops 1258291200 | bytes 12042240 | tf_op jit(solution)/shard_map/bhwc,cd->bhwd/dot_general | solution.py:39
  250.7 5.6 %fusion.48 = f32[3,16,128,320]{2,3,1,0:T(8,128)} fusion(bf16[3,18,130,320]{2,3,1,0:T(8,128)(2,1)S(1)} %bitcast.299, bf16[320,3,3,320]{3,0,2,1:T(8,128)(2,1)S(1)} %copy-done.11), kind=kOutput, calls=%fused_computation.63 | convolution fusion | flops 1258291200 | bytes 12042240 | tf_op jit(solution)/shard_map/bhwc,cd->bhwd/dot_general | solution.py:39
  256.3 5.3 %fusion.50 = f32[3,16,128,320]{2,3,1,0:T(8,128)} fusion(bf16[3,18,130,320]{2,3,1,0:T(8,128)(2,1)S(1)} %bitcast.299, bf16[320,3,3,320]{3,0,2,1:T(8,128)(2,1)S(1)} %copy-done.11), kind=kOutput, calls=%fused_computation.65 | convolution fusion | flops 1258291200 | bytes 12042240 | tf_op jit(solution)/shard_map/bhwc,cd->bhwd/dot_general | solution.py:39
  261.6 6.0 %fusion.52 = f32[3,16,128,320]{2,3,1,0:T(8,128)} fusion(bf16[3,18,130,320]{2,3,1,0:T(8,128)(2,1)S(1)} %bitcast.299, bf16[320,3,3,320]{3,0,2,1:T(8,128)(2,1)S(1)} %copy-done.11), kind=kOutput, calls=%fused_computation.67 | convolution fusion | flops 1258291200 | bytes 12042240 | tf_op jit(solution)/shard_map/bhwc,cd->bhwd/dot_general | solution.py:39
  267.6 5.6 %fusion.54 = f32[3,16,128,320]{2,3,1,0:T(8,128)} fusion(bf16[3,18,130,320]{2,3,1,0:T(8,128)(2,1)S(1)} %bitcast.299, bf16[320,3,3,320]{3,0,2,1:T(8,128)(2,1)S(1)} %copy-done.11), kind=kOutput, calls=%fused_computation.69 | convolution fusion | flops 1258291200 | bytes 12042240 | tf_op jit(solution)/shard_map/bhwc,cd->bhwd/dot_general | solution.py:39
  273.2 5.3 %fusion.56 = f32[3,16,128,320]{2,3,1,0:T(8,128)} fusion(bf16[3,18,130,320]{2,3,1,0:T(8,128)(2,1)S(1)} %bitcast.299, bf16[320,3,3,320]{3,0,2,1:T(8,128)(2,1)S(1)} %copy-done.11), kind=kOutput, calls=%fused_computation.71 | convolution fusion | flops 1258291200 | bytes 12042240 | tf_op jit(solution)/shard_map/bhwc,cd->bhwd/dot_general | solution.py:39
  278.5 28.6 %add_convert_fusion = bf16[3,16,128,320]{2,3,1,0:T(8,128)(2,1)} fusion(f32[3,16,128,320]{2,3,1,0:T(8,128)} %fusion.156, f32[3,16,128,320]{2,3,1,0:T(8,128)} %fusion.42, f32[3,16,128,320]{2,3,1,0:T(8,128)} %fusion.44, f32[3,16,128,320]{2,3,1,0:T(8,128)} %fusion.46, f32[3,16,128,320]{2,3,1,0:T(8,128)} %fusion.48, f32[3,16,128,320]{2,3,1,0:T(8,128)} %fusion.50, ...), kind=kOutput, calls=%fused_computation.28 | convolution fusion | flops 1287782400 | bytes 78892800 | tf_op jit(solution)/shard_map/bhwc,cd->bhwd/dot_general | solution.py:39
  307.2 7.6 %fusion.158 = f32[3,16,128,320]{2,3,1,0:T(8,128)} fusion(bf16[3,16,128,320]{2,3,1,0:T(8,128)(2,1)} %copy-done.3, bf16[320,3,3,320]{3,0,2,1:T(8,128)(2,1)S(1)} %copy-done.9), kind=kOutput, calls=%fused_computation.153 | convolution fusion | flops 1258291200 | bytes 12042240 | tf_op jit(solution)/shard_map/bhwd,cd->bhwc/dot_general | solution.py:54
  314.8 5.3 %fusion.19 = f32[3,16,128,320]{2,3,1,0:T(8,128)} fusion(bf16[3,1,128,320]{2,3,1,0:T(8,128)(2,1)S(1)} %collective-permute-done.3, bf16[3,16,128,320]{2,3,1,0:T(8,128)(2,1)S(1)} %copy-done.4, bf16[320,3,3,320]{3,0,2,1:T(8,128)(2,1)S(1)} %copy-done.9), kind=kOutput, calls=%fused_computation.33 | convolution fusion | flops 1266647040 | bytes 12288000 | tf_op jit(solution)/shard_map/bhwd,cd->bhwc/dot_general | solution.py:54
  320.1 5.3 %fusion.23 = f32[3,16,128,320]{2,3,1,0:T(8,128)} fusion(bf16[3,16,128,320]{2,3,1,0:T(8,128)(2,1)S(1)} %copy-done.4, bf16[3,1,128,320]{2,3,1,0:T(8,128)(2,1)S(1)} %collective-permute-done.2, bf16[320,3,3,320]{3,0,2,1:T(8,128)(2,1)S(1)} %copy-done.9), kind=kOutput, calls=%fused_computation.37 | convolution fusion | flops 1266647040 | bytes 12288000 | tf_op jit(solution)/shard_map/bhwd,cd->bhwc/dot_general | solution.py:54
  325.4 6.3 %fusion.9 = bf16[3,18,130,320]{2,3,1,0:T(8,128)(2,1)S(1)} fusion(bf16[3,1,128,320]{2,3,1,0:T(8,128)(2,1)S(1)} %collective-permute-done.3, bf16[3,16,128,320]{2,3,1,0:T(8,128)(2,1)S(1)} %copy-done.4, bf16[3,1,128,320]{2,3,1,0:T(8,128)(2,1)S(1)} %collective-permute-done.2), kind=kLoop, calls=%fused_computation.15 | loop fusion | flops 26956800 | bytes 8916480 | tf_op jit(solution)/shard_map/concatenate | solution.py:14
  331.8 5.5 %fusion.30 = f32[3,16,128,320]{2,3,1,0:T(8,128)} fusion(bf16[3,18,130,320]{2,3,1,0:T(8,128)(2,1)S(1)} %fusion.9, bf16[320,3,3,320]{3,0,2,1:T(8,128)(2,1)S(1)} %copy-done.9), kind=kOutput, calls=%fused_computation.45 | convolution fusion | flops 1258291200 | bytes 12042240 | tf_op jit(solution)/shard_map/bhwd,cd->bhwc/dot_general | solution.py:54
  337.3 5.3 %fusion.32 = f32[3,16,128,320]{2,3,1,0:T(8,128)} fusion(bf16[3,18,130,320]{2,3,1,0:T(8,128)(2,1)S(1)} %fusion.9, bf16[320,3,3,320]{3,0,2,1:T(8,128)(2,1)S(1)} %copy-done.9), kind=kOutput, calls=%fused_computation.47 | convolution fusion | flops 1258291200 | bytes 12042240 | tf_op jit(solution)/shard_map/bhwd,cd->bhwc/dot_general | solution.py:54
  342.7 5.5 %fusion.34 = f32[3,16,128,320]{2,3,1,0:T(8,128)} fusion(bf16[3,18,130,320]{2,3,1,0:T(8,128)(2,1)S(1)} %fusion.9, bf16[320,3,3,320]{3,0,2,1:T(8,128)(2,1)S(1)} %copy-done.9), kind=kOutput, calls=%fused_computation.49 | convolution fusion | flops 1258291200 | bytes 12042240 | tf_op jit(solution)/shard_map/bhwd,cd->bhwc/dot_general | solution.py:54
  348.2 5.4 %fusion.36 = f32[3,16,128,320]{2,3,1,0:T(8,128)} fusion(bf16[3,18,130,320]{2,3,1,0:T(8,128)(2,1)S(1)} %fusion.9, bf16[320,3,3,320]{3,0,2,1:T(8,128)(2,1)S(1)} %copy-done.9), kind=kOutput, calls=%fused_computation.51 | convolution fusion | flops 1258291200 | bytes 12042240 | tf_op jit(solution)/shard_map/bhwd,cd->bhwc/dot_general | solution.py:54
  353.6 5.5 %fusion.38 = f32[3,16,128,320]{2,3,1,0:T(8,128)} fusion(bf16[3,18,130,320]{2,3,1,0:T(8,128)(2,1)S(1)} %fusion.9, bf16[320,3,3,320]{3,0,2,1:T(8,128)(2,1)S(1)} %copy-done.9), kind=kOutput, calls=%fused_computation.53 | convolution fusion | flops 1258291200 | bytes 12042240 | tf_op jit(solution)/shard_map/bhwd,cd->bhwc/dot_general | solution.py:54
  359.0 5.3 %fusion.28 = f32[3,16,128,320]{2,3,1,0:T(8,128)} fusion(bf16[3,18,130,320]{2,3,1,0:T(8,128)(2,1)S(1)} %fusion.9, bf16[320,3,3,320]{3,0,2,1:T(8,128)(2,1)S(1)} %copy-done.9), kind=kOutput, calls=%fused_computation.43 | convolution fusion | flops 1258291200 | bytes 12042240 | tf_op jit(solution)/shard_map/bhwd,cd->bhwc/dot_general | solution.py:54
  364.4 24.3 %fusion.152 = f32[16,320]{1,0:T(8,128)S(1)} fusion(f32[3,16,128,320]{2,3,1,0:T(8,128)} %fusion.28, f32[3,16,128,320]{2,3,1,0:T(8,128)} %fusion.23, f32[3,16,128,320]{2,3,1,0:T(8,128)} %fusion.30, f32[3,16,128,320]{2,3,1,0:T(8,128)} %fusion.32, f32[3,16,128,320]{2,3,1,0:T(8,128)} %fusion.158, f32[3,16,128,320]{2,3,1,0:T(8,128)} %fusion.34, ...), kind=kOutput, calls=%fused_computation.128 | convolution fusion | flops 393314304 | bytes 70823936 | tf_op jit(solution)/shard_map/bhwr,bhwc->rc/dot_general | solution.py:109
  388.7 57.6 %psum.15 = f32[16,320]{1,0:T(8,128)} all-reduce(f32[16,320]{1,0:T(8,128)S(1)} %fusion.152), channel_id=1, replica_groups=mesh['groups'=2,'mp'=8,'dp'=2] {'mp','dp'}, use_global_device_ids=true, to_apply=%region_2.3 | all-reduce | flops 5120 | bytes 40960 | tf_op jit(solution)/shard_map/psum | solution.py:112
  (76 shorter events, 16.2 us)
Async XLA Ops:
  7.2 62.4 %copy-start = (bf16[1280,320]{0,1:T(8,128)(2,1)S(1)}, bf16[1280,320]{0,1:T(8,128)(2,1)}, u32[]{:S(2)}) copy-start(bf16[1280,320]{0,1:T(8,128)(2,1)} %param.13) | copy-start | bytes 2457604
  7.2 87.5 %all-gather.5.cloned.1.call-start = ((), (), s32[]{:S(2)}) async-start(), calls=%async_computation.2 | async-start | bytes 2488320 | tf_op jit(solution)/shard_map/all_gather | solution.py:93
  7.9 11.8 %copy-start.13 = (bf16[40,320]{1,0:T(8,128)(2,1)S(1)}, bf16[40,320]{1,0:T(8,128)(2,1)}, u32[]{:S(2)}) copy-start(bf16[40,320]{1,0:T(8,128)(2,1)} %param.16) | copy-start | bytes 76804
  7.9 61.5 %copy-start.15 = (s32[3]{0:T(128)S(1)}, s32[3]{0:T(128)}, u32[]{:S(2)}) copy-start(s32[3]{0:T(128)} %param.11) | copy-start | bytes 40
  7.9 220.7 %all-gather.3.cloned.1.call-start = ((), (), s32[]{:S(2)}) async-start(), calls=%async_computation.1 | async-start | bytes 2488320 | tf_op jit(solution)/shard_map/all_gather | solution.py:90
  8.0 3.6 copy-start.5
  11.5 1.9 copy-start.6
  13.5 56.4 %collective-permute-start = (bf16[2,3,1,128,320]{3,4,2,1,0:T(8,128)(2,1)S(1)}, bf16[2,3,1,128,320]{3,4,2,1,0:T(8,128)(2,1)S(1)}, u32[]{:S(2)}, u32[]{:S(2)}) collective-permute-start(bf16[2,3,1,128,320]{3,4,2,1,0:T(8,128)(2,1)S(1)} %get-tuple-element.14), channel_id=1, source_target_pairs={{0,2},{2,4},{4,6},{6,8},{8,10},{10,12},{12,14},{1,3},{3,5},{5,7},{... | collective-permute-start | bytes 1474568 | tf_op jit(solution)/shard_map/ppermute | solution.py:16
  18.3 51.5 %collective-permute-start.1 = (bf16[2,3,1,128,320]{3,4,2,1,0:T(8,128)(2,1)S(1)}, bf16[2,3,1,128,320]{3,4,2,1,0:T(8,128)(2,1)S(1)}, u32[]{:S(2)}, u32[]{:S(2)}) collective-permute-start(bf16[2,3,1,128,320]{3,4,2,1,0:T(8,128)(2,1)S(1)} %get-tuple-element.15), channel_id=1, source_target_pairs={{2,0},{4,2},{6,4},{8,6},{10,8},{12,10},{14,12},{3,1},{5,3},{7,5},{... | collective-permute-start | bytes 1474568 | tf_op jit(solution)/shard_map/ppermute | solution.py:18
  19.7 344.7 %reduce-scatter.4.cloned.1.call-start = ((), (), s32[]{:S(2)}) async-start(), calls=%async_computation.4 | async-start | bytes 4608000
  94.7 9.1 %copy-start.2 = (bf16[3,18,130,320]{2,3,1,0:T(8,128)(2,1)S(1)}, bf16[3,18,130,320]{2,3,1,0:T(8,128)(2,1)}, u32[]{:S(2)}) copy-start(bf16[3,18,130,320]{2,3,1,0:T(8,128)(2,1)} %get-tuple-element.13) | copy-start | bytes 13478404
  94.7 9.1 %copy-start.9 = (bf16[320,3,3,320]{3,0,2,1:T(8,128)(2,1)S(1)}, bf16[320,3,3,320]{3,0,2,1:T(8,128)(2,1)}, u32[]{:S(2)}) copy-start(bf16[320,3,3,320]{3,0,2,1:T(8,128)(2,1)} %all-gather.5.cloned.1.call-done) | copy-start | bytes 5529604
  177.9 28.4 %copy-start.3 = (bf16[3,16,128,320]{2,3,1,0:T(8,128)(2,1)}, bf16[3,16,128,320]{2,3,1,0:T(8,128)(2,1)S(1)}, u32[]{:S(2)}) copy-start(bf16[3,16,128,320]{2,3,1,0:T(8,128)(2,1)S(1)} %multiply_convert_fusion) | copy-start | bytes 11796484
  178.0 14.5 %slice-start.3 = ((s8[8847360]{0:T(1024)(128)(4,1)}), s8[4194304]{0:T(1024)(128)(4,1)S(1)}, s32[]{:S(2)}) async-start(s8[8847360]{0:T(1024)(128)(4,1)} %bitcast.300), calls=%async_computation.8 | async-start | bytes 8388608
  178.0 14.5 %slice-start.4 = ((s8[8847360]{0:T(1024)(128)(4,1)}), s8[4194304]{0:T(1024)(128)(4,1)S(1)}, s32[]{:S(2)}) async-start(s8[8847360]{0:T(1024)(128)(4,1)} %bitcast.300), calls=%async_computation.9 | async-start | bytes 8388608
  183.7 136.3 %collective-permute-start.2 = (bf16[3,1,128,320]{2,3,1,0:T(8,128)(2,1)S(1)}, bf16[3,1,128,320]{2,3,1,0:T(8,128)(2,1)S(1)}, u32[]{:S(2)}, u32[]{:S(2)}) collective-permute-start(bf16[3,1,128,320]{2,3,1,0:T(8,128)(2,1)S(1)} %get-tuple-element.16), channel_id=1, source_target_pairs={{0,2},{2,4},{4,6},{6,8},{8,10},{10,12},{12,14},{1,3},{3,5},{5,7},{... | collective-permute-start | bytes 737288 | tf_op jit(solution)/shard_map/ppermute | solution.py:16
  185.1 7.5 %slice-start.5 = ((s8[8847360]{0:T(1024)(128)(4,1)}), s8[458752]{0:T(1024)(128)(4,1)S(1)}, s32[]{:S(2)}) async-start(s8[8847360]{0:T(1024)(128)(4,1)} %bitcast.300), calls=%async_computation.10 | async-start | bytes 917504
  185.1 129.7 %collective-permute-start.3 = (bf16[3,1,128,320]{2,3,1,0:T(8,128)(2,1)S(1)}, bf16[3,1,128,320]{2,3,1,0:T(8,128)(2,1)S(1)}, u32[]{:S(2)}, u32[]{:S(2)}) collective-permute-start(bf16[3,1,128,320]{2,3,1,0:T(8,128)(2,1)S(1)} %get-tuple-element.17), channel_id=1, source_target_pairs={{2,0},{4,2},{6,4},{8,6},{10,8},{12,10},{14,12},{3,1},{5,3},{7,5},{... | collective-permute-start | bytes 737288 | tf_op jit(solution)/shard_map/ppermute | solution.py:18
  208.6 2.2 copy-start.10
  216.4 7.6 %copy-start.7 = (bf16[3,16,128,320]{2,3,1,0:T(8,128)(2,1)S(1)}, bf16[3,16,128,320]{2,3,1,0:T(8,128)(2,1)}, u32[]{:S(2)}) copy-start(bf16[3,16,128,320]{2,3,1,0:T(8,128)(2,1)} %get-tuple-element.20) | copy-start | bytes 11796484
  216.4 7.6 %copy-start.14 = (bf16[3,16,128,320]{2,3,1,0:T(8,128)(2,1)S(1)}, bf16[3,16,128,320]{2,3,1,0:T(8,128)(2,1)}, u32[]{:S(2)}) copy-start(bf16[3,16,128,320]{2,3,1,0:T(8,128)(2,1)} %param.17) | copy-start | bytes 11796484
  224.0 2.2 copy-start.8
  228.6 217.7 %all-reduce.5.cloned.1.call-start = ((), (), s32[]{:S(2)}) async-start(), calls=%async_computation.3 | async-start | bytes 1024000 | tf_op jit(solution)/shard_map/psum | solution.py:128
  228.7 9.0 %copy-start.11 = (bf16[320,3,3,320]{3,0,2,1:T(8,128)(2,1)S(1)}, bf16[320,3,3,320]{3,0,2,1:T(8,128)(2,1)}, u32[]{:S(2)}) copy-start(bf16[320,3,3,320]{3,0,2,1:T(8,128)(2,1)} %all-gather.3.cloned.1.call-done) | copy-start | bytes 5529604
  228.7 16.5 %slice-start = ((s8[8847360]{0:T(1024)(128)(4,1)}), s8[4194304]{0:T(1024)(128)(4,1)S(1)}, s32[]{:S(2)}) async-start(s8[8847360]{0:T(1024)(128)(4,1)} %bitcast.298), calls=%async_computation.5 | async-start | bytes 8388608
  228.7 16.5 %slice-start.1 = ((s8[8847360]{0:T(1024)(128)(4,1)}), s8[4194304]{0:T(1024)(128)(4,1)S(1)}, s32[]{:S(2)}) async-start(s8[8847360]{0:T(1024)(128)(4,1)} %bitcast.298), calls=%async_computation.6 | async-start | bytes 8388608
  237.7 7.5 %slice-start.2 = ((s8[8847360]{0:T(1024)(128)(4,1)}), s8[458752]{0:T(1024)(128)(4,1)S(1)}, s32[]{:S(2)}) async-start(s8[8847360]{0:T(1024)(128)(4,1)} %bitcast.298), calls=%async_computation.7 | async-start | bytes 917504
  307.2 7.6 %copy-start.4 = (bf16[3,16,128,320]{2,3,1,0:T(8,128)(2,1)S(1)}, bf16[3,16,128,320]{2,3,1,0:T(8,128)(2,1)}, u32[]{:S(2)}) copy-start(bf16[3,16,128,320]{2,3,1,0:T(8,128)(2,1)} %copy-done.3) | copy-start | bytes 11796484
  359.0 5.4 %copy-start.12 = (s32[3,16,128]{2,1,0:T(8,128)S(1)}, s32[3,16,128]{2,1,0:T(8,128)}, u32[]{:S(2)}) copy-start(s32[3,16,128]{2,1,0:T(8,128)} %param.10) | copy-start | bytes 73732
  364.4 85.8 %copy-start.1 = (bf16[1280,320]{0,1:T(8,128)(2,1)S(1)}, bf16[1280,320]{0,1:T(8,128)(2,1)}, u32[]{:S(2)}) copy-start(bf16[1280,320]{0,1:T(8,128)(2,1)} %param.13) | copy-start | bytes 2457604
Sparse Core Ops, SparseCore 0:
  10.2 66.9 all-gather.4
  79.4 49.2 all-gather.2
  228.7 87.1 reduce-scatter.3
  364.5 20.1 all-reduce.4
where the time goes:
time: 461 us; the launch traced here: 457 us
  matrix products  278 us (60%)
  blocking collectives  107 us (23%)
  other arithmetic  27.1 us (6%)
  local copies, waits for them, and re-layouts  20.2 us (4%)
  between operations  14.4 us (3%)
  starting transfers between devices  9.53 us (2%)
    dot_general x18, matrix products, forward_taps(): jnp.einsum('bhwc,cd->bhwd', frame[:, tap_row:tap_row + row_count, tap_col...  154 us
    psum x1, blocking collectives, per_device(): grad_table = lax.psum(table_local, ('mp', 'dp'))  57.6 us
    dot_general x9, matrix products, backward_taps(): jnp.einsum('bhwd,cd->bhwc', frame[:, 2 - tap_row:2 - tap_row + row_count,...  50.8 us
    all_gather x1, blocking collectives, per_device(): lax.all_gather(mix_weight, 'mp', axis=0, tiled=True)  49.6 us
    dot_general x9, matrix products, per_device(): jnp.einsum('bhwc,bhwd->cd', control_frame[:, tap_row:tap_row + row_count,...  27.3 us
    concatenate x2, other arithmetic, with_halo(): jnp.concatenate([lax.ppermute(tail, axis, [(i, (i + 1) % count) for i in...  24.5 us
    dot_general x1, matrix products, per_device(): jnp.einsum('bhwr,bhwc->rc', onehot.astype(jnp.float32), back_in, precisio...  24.3 us
  transfers between devices with their start and end apart: 8, of which 0 were waited for; matrix products, arithmetic and copies ran while one was open for 69% of the time, Pallas kernels for 0%

commit v1 on v0

--- a/solution.py
+++ b/solution.py
@@ -109,7 +109,7 @@
     table_local = jnp.einsum(
         "bhwr,bhwc->rc", onehot.astype(jnp.float32), back_in, precision=lax.Precision.HIGHEST
     )
-    grad_table = lax.psum(table_local, ("mp", "dp"))
+    grad_table = jnp.sum(lax.all_gather(table_local, ("mp", "dp")), axis=0)
     pieces = []
     for tap_row in range(3):
         for tap_col in range(3):

time: 461 us -> 426 us (0.924)
  blocking collectives: 107 us -> 71.8 us
    psum x1 -> x0, blocking collectives: 57.6 us -> none  [per_device(): grad_table = lax.psum(table_local, ('mp', 'dp'))]
    all_gather x0 -> x1, blocking collectives: none -> 22.2 us  [per_device(): grad_table = jnp.sum(lax.all_gather(table_local, ('mp', 'dp')), axis=0)]
  transfers between devices with their start and end apart: 8 -> 8, of which waited for: 0 -> 0; matrix products, arithmetic and copies ran while one was open for 69% -> 75% of each run, Pallas kernels for 0% -> 0%
where the time goes in v1:
time: 426 us; the launch traced here: 422 us
  matrix products  278 us (65%)
  blocking collectives  71.8 us (17%)
  other arithmetic  27.7 us (7%)
  local copies, waits for them, and re-layouts  20.2 us (5%)
  between operations  14.5 us (3%)
  starting transfers between devices  9.53 us (2%)
    dot_general x18, matrix products, forward_taps(): jnp.einsum('bhwc,cd->bhwd', frame[:, tap_row:tap_row + row_count, tap_col...  154 us
    dot_general x9, matrix products, backward_taps(): jnp.einsum('bhwd,cd->bhwc', frame[:, 2 - tap_row:2 - tap_row + row_count,...  50.8 us
    all_gather x1, blocking collectives, per_device(): lax.all_gather(mix_weight, 'mp', axis=0, tiled=True)  49.6 us
    dot_general x9, matrix products, per_device(): jnp.einsum('bhwc,bhwd->cd', control_frame[:, tap_row:tap_row + row_count,...  27.3 us
    concatenate x2, other arithmetic, with_halo(): jnp.concatenate([lax.ppermute(tail, axis, [(i, (i + 1) % count) for i in...  24.5 us
    dot_general x1, matrix products, per_device(): jnp.einsum('bhwr,bhwc->rc', onehot.astype(jnp.float32), back_in, precisio...  24.3 us
    all_gather x1, blocking collectives, per_device(): grad_table = jnp.sum(lax.all_gather(table_local, ('mp', 'dp')), axis=0)  22.2 us
  transfers between devices with their start and end apart: 8, of which 0 were waited for; matrix products, arithmetic and copies ran while one was open for 75% of the time, Pallas kernels for 0%

profile of v1, /device:TPU:0, one launch (start us, length us, event | category | flops | bytes accessed | tf_op | source)
XLA Modules:
  0.0 422.1 jit_solution(12087852666114908139)
XLA Ops:
  8.0 3.5 fusion.27
  13.5 4.9 %collective-permute-start = (bf16[2,3,1,128,320]{3,4,2,1,0:T(8,128)(2,1)S(1)}, bf16[2,3,1,128,320]{3,4,2,1,0:T(8,128)(2,1)S(1)}, u32[]{:S(2)}, u32[]{:S(2)}) collective-permute-start(bf16[2,3,1,128,320]{3,4,2,1,0:T(8,128)(2,1)S(1)} %get-tuple-element.14), channel_id=1, source_target_pairs={{0,2},{2,4},{4,6},{6,8},{8,10},{10,12},{12,14},{1,3},{3,5},{5,7},{... | collective-permute-start | bytes 1474568 | tf_op jit(solution)/shard_map/ppermute | solution.py:16
  19.7 49.6 %all_gather.18 = bf16[320,320]{1,0:T(8,128)(2,1)S(1)} all-gather(bf16[40,320]{1,0:T(8,128)(2,1)S(1)} %copy-done.13), channel_id=1, replica_groups=mesh['groups'=2,'mp'=8,'dp'=2] {'mp'}, dimensions={0}, use_global_device_ids=true | all-gather | bytes 230400 | tf_op jit(solution)/shard_map/all_gather | solution.py:94
  69.9 18.2 %select_maximum_fusion = bf16[2,3,18,130,320]{3,4,2,1,0:T(8,128)(2,1)S(1)} fusion(bf16[2,3,1,128,320]{3,4,2,1,0:T(8,128)(2,1)S(1)} %collective-permute-done.1, bf16[2,3,1,128,320]{3,4,2,1,0:T(8,128)(2,1)S(1)} %collective-permute-done, bf16[1,3,16,128,320]{3,4,2,1,0:T(8,128)(2,1)} %copy-done.6, bf16[1,3,16,128,320]{3,4,2,1,0:T(8,128)(2,1)} %bitcast.303), kind=kLoop, calls=%fused_computation.5 | loop fusion | flops 67392000 | bytes 17832960 | tf_op jit(solution)/shard_map/concatenate | solution.py:14
  88.1 6.6 %slice_bitcast_fusion.1 = (bf16[3,18,130,320]{2,3,1,0:T(8,128)(2,1)}, bf16[3,18,130,320]{2,3,1,0:T(8,128)(2,1)}) fusion(bf16[2,3,18,130,320]{3,4,2,1,0:T(8,128)(2,1)S(1)} %select_maximum_fusion), kind=kLoop, calls=%fused_computation.17 | loop fusion | bytes 17971200 | tf_op jit(solution)/shard_map/squeeze | solution.py:84
  94.7 9.1 %fusion.64 = f32[3,16,128,320]{2,3,1,0:T(8,128)} fusion(bf16[3,18,130,320]{2,3,1,0:T(8,128)(2,1)} %get-tuple-element.13, bf16[320,3,3,320]{3,0,2,1:T(8,128)(2,1)} %all-gather.6.cloned.1.call-done), kind=kOutput, calls=%fused_computation.79 | convolution fusion | flops 1258291200 | bytes 12042240 | tf_op jit(solution)/shard_map/bhwc,cd->bhwd/dot_general | solution.py:39
  103.8 5.3 %fusion.68 = f32[3,16,128,320]{2,3,1,0:T(8,128)} fusion(bf16[3,18,130,320]{2,3,1,0:T(8,128)(2,1)S(1)} %copy-done.2, bf16[320,3,3,320]{3,0,2,1:T(8,128)(2,1)S(1)} %copy-done.9), kind=kOutput, calls=%fused_computation.83 | convolution fusion | flops 1258291200 | bytes 12042240 | tf_op jit(solution)/shard_map/bhwc,cd->bhwd/dot_general | solution.py:39
  109.1 5.5 %fusion.72 = f32[3,16,128,320]{2,3,1,0:T(8,128)} fusion(bf16[3,18,130,320]{2,3,1,0:T(8,128)(2,1)S(1)} %copy-done.2, bf16[320,3,3,320]{3,0,2,1:T(8,128)(2,1)S(1)} %copy-done.9), kind=kOutput, calls=%fused_computation.87 | convolution fusion | flops 1258291200 | bytes 12042240 | tf_op jit(solution)/shard_map/bhwc,cd->bhwd/dot_general | solution.py:39
  114.6 5.5 %fusion.76 = f32[3,16,128,320]{2,3,1,0:T(8,128)} fusion(bf16[3,18,130,320]{2,3,1,0:T(8,128)(2,1)S(1)} %copy-done.2, bf16[320,3,3,320]{3,0,2,1:T(8,128)(2,1)S(1)} %copy-done.9), kind=kOutput, calls=%fused_computation.91 | convolution fusion | flops 1258291200 | bytes 12042240 | tf_op jit(solution)/shard_map/bhwc,cd->bhwd/dot_general | solution.py:39
  120.2 5.3 %fusion.80 = f32[3,16,128,320]{2,3,1,0:T(8,128)} fusion(bf16[3,18,130,320]{2,3,1,0:T(8,128)(2,1)S(1)} %copy-done.2, bf16[320,3,3,320]{3,0,2,1:T(8,128)(2,1)S(1)} %copy-done.9), kind=kOutput, calls=%fused_computation.95 | convolution fusion | flops 1258291200 | bytes 12042240 | tf_op jit(solution)/shard_map/bhwc,cd->bhwd/dot_general | solution.py:39
  125.5 5.8 %fusion.84 = f32[3,16,128,320]{2,3,1,0:T(8,128)} fusion(bf16[3,18,130,320]{2,3,1,0:T(8,128)(2,1)S(1)} %copy-done.2, bf16[320,3,3,320]{3,0,2,1:T(8,128)(2,1)S(1)} %copy-done.9), kind=kOutput, calls=%fused_computation.99 | convolution fusion | flops 1258291200 | bytes 12042240 | tf_op jit(solution)/shard_map/bhwc,cd->bhwd/dot_general | solution.py:39
  131.3 5.7 %fusion.88 = f32[3,16,128,320]{2,3,1,0:T(8,128)} fusion(bf16[3,18,130,320]{2,3,1,0:T(8,128)(2,1)S(1)} %copy-done.2, bf16[320,3,3,320]{3,0,2,1:T(8,128)(2,1)S(1)} %copy-done.9), kind=kOutput, calls=%fused_computation.103 | convolution fusion | flops 1258291200 | bytes 12042240 | tf_op jit(solution)/shard_map/bhwc,cd->bhwd/dot_general | solution.py:39
  137.0 5.4 %fusion.92 = f32[3,16,128,320]{2,3,1,0:T(8,128)} fusion(bf16[3,18,130,320]{2,3,1,0:T(8,128)(2,1)S(1)} %copy-done.2, bf16[320,3,3,320]{3,0,2,1:T(8,128)(2,1)S(1)} %copy-done.9), kind=kOutput, calls=%fused_computation.107 | convolution fusion | flops 1258291200 | bytes 12042240 | tf_op jit(solution)/shard_map/bhwc,cd->bhwd/dot_general | solution.py:39
  142.4 28.2 %multiply_convert_fusion.1 = (bf16[3,16,128,320]{2,3,1,0:T(8,128)(2,1)}, f32[3,16,128,320]{2,3,1,0:T(8,128)}) fusion(f32[3,320]{1,0:T(4,128)S(1)} %fusion.163, bf16[3,18,130,320]{2,3,1,0:T(8,128)(2,1)} %get-tuple-element.13, bf16[320,3,3,320]{3,0,2,1:T(8,128)(2,1)S(1)} %copy-done.9, f32[3,16,128,320]{2,3,1,0:T(8,128)} %fusion.64, ...), kind=kOutput, calls=%fused_computation.29 | convolution fusion | flops 1285816320 | bytes 78895104 | tf_op jit(solution)/shard_map/bhwc,cd->bhwd/dot_general | solution.py:39
  170.6 7.3 %multiply_convert_fusion = bf16[3,16,128,320]{2,3,1,0:T(8,128)(2,1)S(1)} fusion(f32[3,16,128,320]{2,3,1,0:T(8,128)} %get-tuple-element.21, bf16[3,16,128,320]{2,3,1,0:T(8,128)(2,1)} %param.17, bf16[320,320]{1,0:T(8,128)(2,1)S(1)} %all_gather.18), kind=kOutput, calls=%fused_computation.27 | convolution fusion | flops 1275985920 | bytes 15933440 | tf_op jit(solution)/shard_map/bhwd,cd->bhwc/dot_general | solution.py:100
  178.0 5.7 %fusion.101 = f32[320,9,320]{0,2,1:T(8,128)S(1)} fusion(bf16[3,16,128,320]{2,3,1,0:T(8,128)(2,1)S(1)} %multiply_convert_fusion, bf16[3,18,130,320]{2,3,1,0:T(8,128)(2,1)} %get-tuple-element.13), kind=kOutput, calls=%fused_computation.110 | convolution fusion | flops 1258291200 | bytes 8355840 | tf_op jit(solution)/shard_map/bhwc,bhwd->cd/dot_general | solution.py:117
  187.0 5.5 %fusion.107 = f32[320,9,320]{0,2,1:T(8,128)S(1)} fusion(f32[320,9,320]{0,2,1:T(8,128)S(1)} %fusion.101, bf16[3,16,128,320]{2,3,1,0:T(8,128)(2,1)S(1)} %multiply_convert_fusion, bf16[3,18,130,320]{2,3,1,0:T(8,128)(2,1)} %get-tuple-element.13), kind=kOutput, calls=%fused_computation.112 | convolution fusion | flops 1258291200 | bytes 8355840 | tf_op jit(solution)/shard_map/bhwc,bhwd->cd/dot_general | solution.py:117
  192.5 2.3 fusion.113
  194.8 2.2 fusion.119
  197.0 2.3 fusion.125
  199.3 2.3 fusion.131
  201.6 2.2 fusion.137
  203.8 2.5 fusion.143
  206.3 2.3 fusion.149
  210.8 5.6 %copy.38 = f32[320,2880]{1,0:T(8,128)} copy(f32[320,2880]{0,1:T(8,128)} %bitcast.305) | data formatting | bytes 7372800 | tf_op jit(solution)/shard_map/reshape | solution.py:124
  216.4 7.6 %fusion.156 = f32[3,16,128,320]{2,3,1,0:T(8,128)} fusion(bf16[3,16,128,320]{2,3,1,0:T(8,128)(2,1)} %get-tuple-element.20, bf16[320,320]{1,0:T(8,128)(2,1)S(1)} %all_gather.18), kind=kOutput, calls=%fused_computation.151 | convolution fusion | flops 1258291200 | bytes 12001280 | tf_op jit(solution)/shard_map/bhwc,cd->bhwd/dot_general | solution.py:98
  226.2 2.3 pad_maximum_fusion
  228.7 9.0 %fusion.42 = f32[3,16,128,320]{2,3,1,0:T(8,128)} fusion(bf16[3,18,130,320]{2,3,1,0:T(8,128)(2,1)} %get-tuple-element.12, bf16[320,3,3,320]{3,0,2,1:T(8,128)(2,1)} %all-gather.4.cloned.1.call-done), kind=kOutput, calls=%fused_computation.57 | convolution fusion | flops 1258291200 | bytes 12042240 | tf_op jit(solution)/shard_map/bhwc,cd->bhwd/dot_general | solution.py:39
  237.7 7.5 %fusion.44 = f32[3,16,128,320]{2,3,1,0:T(8,128)} fusion(bf16[3,18,130,320]{2,3,1,0:T(8,128)(2,1)} %get-tuple-element.12, bf16[320,3,3,320]{3,0,2,1:T(8,128)(2,1)S(1)} %copy-done.11), kind=kOutput, calls=%fused_computation.59 | convolution fusion | flops 1258291200 | bytes 12042240 | tf_op jit(solution)/shard_map/bhwc,cd->bhwd/dot_general | solution.py:39
  245.2 5.5 %fusion.46 = f32[3,16,128,320]{2,3,1,0:T(8,128)} fusion(bf16[3,18,130,320]{2,3,1,0:T(8,128)(2,1)S(1)} %bitcast.300, bf16[320,3,3,320]{3,0,2,1:T(8,128)(2,1)S(1)} %copy-done.11), kind=kOutput, calls=%fused_computation.61 | convolution fusion | flops 1258291200 | bytes 12042240 | tf_op jit(solution)/shard_map/bhwc,cd->bhwd/dot_general | solution.py:39
  250.7 5.6 %fusion.48 = f32[3,16,128,320]{2,3,1,0:T(8,128)} fusion(bf16[3,18,130,320]{2,3,1,0:T(8,128)(2,1)S(1)} %bitcast.300, bf16[320,3,3,320]{3,0,2,1:T(8,128)(2,1)S(1)} %copy-done.11), kind=kOutput, calls=%fused_computation.63 | convolution fusion | flops 1258291200 | bytes 12042240 | tf_op jit(solution)/shard_map/bhwc,cd->bhwd/dot_general | solution.py:39
  256.3 5.3 %fusion.50 = f32[3,16,128,320]{2,3,1,0:T(8,128)} fusion(bf16[3,18,130,320]{2,3,1,0:T(8,128)(2,1)S(1)} %bitcast.300, bf16[320,3,3,320]{3,0,2,1:T(8,128)(2,1)S(1)} %copy-done.11), kind=kOutput, calls=%fused_computation.65 | convolution fusion | flops 1258291200 | bytes 12042240 | tf_op jit(solution)/shard_map/bhwc,cd->bhwd/dot_general | solution.py:39
  261.6 6.0 %fusion.52 = f32[3,16,128,320]{2,3,1,0:T(8,128)} fusion(bf16[3,18,130,320]{2,3,1,0:T(8,128)(2,1)S(1)} %bitcast.300, bf16[320,3,3,320]{3,0,2,1:T(8,128)(2,1)S(1)} %copy-done.11), kind=kOutput, calls=%fused_computation.67 | convolution fusion | flops 1258291200 | bytes 12042240 | tf_op jit(solution)/shard_map/bhwc,cd->bhwd/dot_general | solution.py:39
  267.6 5.6 %fusion.54 = f32[3,16,128,320]{2,3,1,0:T(8,128)} fusion(bf16[3,18,130,320]{2,3,1,0:T(8,128)(2,1)S(1)} %bitcast.300, bf16[320,3,3,320]{3,0,2,1:T(8,128)(2,1)S(1)} %copy-done.11), kind=kOutput, calls=%fused_computation.69 | convolution fusion | flops 1258291200 | bytes 12042240 | tf_op jit(solution)/shard_map/bhwc,cd->bhwd/dot_general | solution.py:39
  273.2 5.3 %fusion.56 = f32[3,16,128,320]{2,3,1,0:T(8,128)} fusion(bf16[3,18,130,320]{2,3,1,0:T(8,128)(2,1)S(1)} %bitcast.300, bf16[320,3,3,320]{3,0,2,1:T(8,128)(2,1)S(1)} %copy-done.11), kind=kOutput, calls=%fused_computation.71 | convolution fusion | flops 1258291200 | bytes 12042240 | tf_op jit(solution)/shard_map/bhwc,cd->bhwd/dot_general | solution.py:39
  278.5 28.6 %add_convert_fusion = bf16[3,16,128,320]{2,3,1,0:T(8,128)(2,1)} fusion(f32[3,16,128,320]{2,3,1,0:T(8,128)} %fusion.156, f32[3,16,128,320]{2,3,1,0:T(8,128)} %fusion.42, f32[3,16,128,320]{2,3,1,0:T(8,128)} %fusion.44, f32[3,16,128,320]{2,3,1,0:T(8,128)} %fusion.46, f32[3,16,128,320]{2,3,1,0:T(8,128)} %fusion.48, f32[3,16,128,320]{2,3,1,0:T(8,128)} %fusion.50, ...), kind=kOutput, calls=%fused_computation.28 | convolution fusion | flops 1287782400 | bytes 78892800 | tf_op jit(solution)/shard_map/bhwc,cd->bhwd/dot_general | solution.py:39
  307.2 7.6 %fusion.158 = f32[3,16,128,320]{2,3,1,0:T(8,128)} fusion(bf16[3,16,128,320]{2,3,1,0:T(8,128)(2,1)} %copy-done.3, bf16[320,3,3,320]{3,0,2,1:T(8,128)(2,1)S(1)} %copy-done.9), kind=kOutput, calls=%fused_computation.153 | convolution fusion | flops 1258291200 | bytes 12042240 | tf_op jit(solution)/shard_map/bhwd,cd->bhwc/dot_general | solution.py:54
  314.8 5.3 %fusion.19 = f32[3,16,128,320]{2,3,1,0:T(8,128)} fusion(bf16[3,1,128,320]{2,3,1,0:T(8,128)(2,1)S(1)} %collective-permute-done.3, bf16[3,16,128,320]{2,3,1,0:T(8,128)(2,1)S(1)} %copy-done.4, bf16[320,3,3,320]{3,0,2,1:T(8,128)(2,1)S(1)} %copy-done.9), kind=kOutput, calls=%fused_computation.33 | convolution fusion | flops 1266647040 | bytes 12288000 | tf_op jit(solution)/shard_map/bhwd,cd->bhwc/dot_general | solution.py:54
  320.1 5.3 %fusion.23 = f32[3,16,128,320]{2,3,1,0:T(8,128)} fusion(bf16[3,16,128,320]{2,3,1,0:T(8,128)(2,1)S(1)} %copy-done.4, bf16[3,1,128,320]{2,3,1,0:T(8,128)(2,1)S(1)} %collective-permute-done.2, bf16[320,3,3,320]{3,0,2,1:T(8,128)(2,1)S(1)} %copy-done.9), kind=kOutput, calls=%fused_computation.37 | convolution fusion | flops 1266647040 | bytes 12288000 | tf_op jit(solution)/shard_map/bhwd,cd->bhwc/dot_general | solution.py:54
  325.4 6.3 %fusion.9 = bf16[3,18,130,320]{2,3,1,0:T(8,128)(2,1)S(1)} fusion(bf16[3,1,128,320]{2,3,1,0:T(8,128)(2,1)S(1)} %collective-permute-done.3, bf16[3,16,128,320]{2,3,1,0:T(8,128)(2,1)S(1)} %copy-done.4, bf16[3,1,128,320]{2,3,1,0:T(8,128)(2,1)S(1)} %collective-permute-done.2), kind=kLoop, calls=%fused_computation.15 | loop fusion | flops 26956800 | bytes 8916480 | tf_op jit(solution)/shard_map/concatenate | solution.py:14
  331.8 5.5 %fusion.30 = f32[3,16,128,320]{2,3,1,0:T(8,128)} fusion(bf16[3,18,130,320]{2,3,1,0:T(8,128)(2,1)S(1)} %fusion.9, bf16[320,3,3,320]{3,0,2,1:T(8,128)(2,1)S(1)} %copy-done.9), kind=kOutput, calls=%fused_computation.45 | convolution fusion | flops 1258291200 | bytes 12042240 | tf_op jit(solution)/shard_map/bhwd,cd->bhwc/dot_general | solution.py:54
  337.3 5.3 %fusion.32 = f32[3,16,128,320]{2,3,1,0:T(8,128)} fusion(bf16[3,18,130,320]{2,3,1,0:T(8,128)(2,1)S(1)} %fusion.9, bf16[320,3,3,320]{3,0,2,1:T(8,128)(2,1)S(1)} %copy-done.9), kind=kOutput, calls=%fused_computation.47 | convolution fusion | flops 1258291200 | bytes 12042240 | tf_op jit(solution)/shard_map/bhwd,cd->bhwc/dot_general | solution.py:54
  342.7 5.5 %fusion.34 = f32[3,16,128,320]{2,3,1,0:T(8,128)} fusion(bf16[3,18,130,320]{2,3,1,0:T(8,128)(2,1)S(1)} %fusion.9, bf16[320,3,3,320]{3,0,2,1:T(8,128)(2,1)S(1)} %copy-done.9), kind=kOutput, calls=%fused_computation.49 | convolution fusion | flops 1258291200 | bytes 12042240 | tf_op jit(solution)/shard_map/bhwd,cd->bhwc/dot_general | solution.py:54
  348.2 5.4 %fusion.36 = f32[3,16,128,320]{2,3,1,0:T(8,128)} fusion(bf16[3,18,130,320]{2,3,1,0:T(8,128)(2,1)S(1)} %fusion.9, bf16[320,3,3,320]{3,0,2,1:T(8,128)(2,1)S(1)} %copy-done.9), kind=kOutput, calls=%fused_computation.51 | convolution fusion | flops 1258291200 | bytes 12042240 | tf_op jit(solution)/shard_map/bhwd,cd->bhwc/dot_general | solution.py:54
  353.6 5.5 %fusion.38 = f32[3,16,128,320]{2,3,1,0:T(8,128)} fusion(bf16[3,18,130,320]{2,3,1,0:T(8,128)(2,1)S(1)} %fusion.9, bf16[320,3,3,320]{3,0,2,1:T(8,128)(2,1)S(1)} %copy-done.9), kind=kOutput, calls=%fused_computation.53 | convolution fusion | flops 1258291200 | bytes 12042240 | tf_op jit(solution)/shard_map/bhwd,cd->bhwc/dot_general | solution.py:54
  359.0 5.3 %fusion.28 = f32[3,16,128,320]{2,3,1,0:T(8,128)} fusion(bf16[3,18,130,320]{2,3,1,0:T(8,128)(2,1)S(1)} %fusion.9, bf16[320,3,3,320]{3,0,2,1:T(8,128)(2,1)S(1)} %copy-done.9), kind=kOutput, calls=%fused_computation.43 | convolution fusion | flops 1258291200 | bytes 12042240 | tf_op jit(solution)/shard_map/bhwd,cd->bhwc/dot_general | solution.py:54
  364.4 24.3 %fusion.152 = f32[16,320]{1,0:T(8,128)S(1)} fusion(f32[3,16,128,320]{2,3,1,0:T(8,128)} %fusion.28, f32[3,16,128,320]{2,3,1,0:T(8,128)} %fusion.23, f32[3,16,128,320]{2,3,1,0:T(8,128)} %fusion.30, f32[3,16,128,320]{2,3,1,0:T(8,128)} %fusion.32, f32[3,16,128,320]{2,3,1,0:T(8,128)} %fusion.158, f32[3,16,128,320]{2,3,1,0:T(8,128)} %fusion.34, ...), kind=kOutput, calls=%fused_computation.128 | convolution fusion | flops 393314304 | bytes 70823936 | tf_op jit(solution)/shard_map/bhwr,bhwc->rc/dot_general | solution.py:109
  388.7 22.2 %all-gather = f32[256,320]{1,0:T(8,128)S(1)} all-gather(f32[16,320]{1,0:T(8,128)S(1)} %fusion.152), channel_id=2, replica_groups=mesh['groups'=2,'mp'=8,'dp'=2] {'mp','dp'}, dimensions={0}, use_global_device_ids=true | all-gather | bytes 348160 | tf_op jit(solution)/shard_map/all_gather | solution.py:112
  (77 shorter events, 16.8 us)
Async XLA Ops:
  7.2 62.4 %copy-start = (bf16[1280,320]{0,1:T(8,128)(2,1)S(1)}, bf16[1280,320]{0,1:T(8,128)(2,1)}, u32[]{:S(2)}) copy-start(bf16[1280,320]{0,1:T(8,128)(2,1)} %param.13) | copy-start | bytes 2457604
  7.2 87.5 %all-gather.6.cloned.1.call-start = ((), (), s32[]{:S(2)}) async-start(), calls=%async_computation.2 | async-start | bytes 2488320 | tf_op jit(solution)/shard_map/all_gather | solution.py:93
  7.9 11.8 %copy-start.13 = (bf16[40,320]{1,0:T(8,128)(2,1)S(1)}, bf16[40,320]{1,0:T(8,128)(2,1)}, u32[]{:S(2)}) copy-start(bf16[40,320]{1,0:T(8,128)(2,1)} %param.16) | copy-start | bytes 76804
  7.9 61.5 %copy-start.15 = (s32[3]{0:T(128)S(1)}, s32[3]{0:T(128)}, u32[]{:S(2)}) copy-start(s32[3]{0:T(128)} %param.11) | copy-start | bytes 40
  7.9 220.7 %all-gather.4.cloned.1.call-start = ((), (), s32[]{:S(2)}) async-start(), calls=%async_computation.1 | async-start | bytes 2488320 | tf_op jit(solution)/shard_map/all_gather | solution.py:90
  8.0 3.6 copy-start.5
  11.5 1.9 copy-start.6
  13.5 56.4 %collective-permute-start = (bf16[2,3,1,128,320]{3,4,2,1,0:T(8,128)(2,1)S(1)}, bf16[2,3,1,128,320]{3,4,2,1,0:T(8,128)(2,1)S(1)}, u32[]{:S(2)}, u32[]{:S(2)}) collective-permute-start(bf16[2,3,1,128,320]{3,4,2,1,0:T(8,128)(2,1)S(1)} %get-tuple-element.14), channel_id=1, source_target_pairs={{0,2},{2,4},{4,6},{6,8},{8,10},{10,12},{12,14},{1,3},{3,5},{5,7},{... | collective-permute-start | bytes 1474568 | tf_op jit(solution)/shard_map/ppermute | solution.py:16
  18.3 51.5 %collective-permute-start.1 = (bf16[2,3,1,128,320]{3,4,2,1,0:T(8,128)(2,1)S(1)}, bf16[2,3,1,128,320]{3,4,2,1,0:T(8,128)(2,1)S(1)}, u32[]{:S(2)}, u32[]{:S(2)}) collective-permute-start(bf16[2,3,1,128,320]{3,4,2,1,0:T(8,128)(2,1)S(1)} %get-tuple-element.15), channel_id=1, source_target_pairs={{2,0},{4,2},{6,4},{8,6},{10,8},{12,10},{14,12},{3,1},{5,3},{7,5},{... | collective-permute-start | bytes 1474568 | tf_op jit(solution)/shard_map/ppermute | solution.py:18
  19.7 344.7 %reduce-scatter.4.cloned.1.call-start = ((), (), s32[]{:S(2)}) async-start(), calls=%async_computation.4 | async-start | bytes 4608000
  94.7 9.1 %copy-start.2 = (bf16[3,18,130,320]{2,3,1,0:T(8,128)(2,1)S(1)}, bf16[3,18,130,320]{2,3,1,0:T(8,128)(2,1)}, u32[]{:S(2)}) copy-start(bf16[3,18,130,320]{2,3,1,0:T(8,128)(2,1)} %get-tuple-element.13) | copy-start | bytes 13478404
  94.7 9.1 %copy-start.9 = (bf16[320,3,3,320]{3,0,2,1:T(8,128)(2,1)S(1)}, bf16[320,3,3,320]{3,0,2,1:T(8,128)(2,1)}, u32[]{:S(2)}) copy-start(bf16[320,3,3,320]{3,0,2,1:T(8,128)(2,1)} %all-gather.6.cloned.1.call-done) | copy-start | bytes 5529604
  177.9 28.4 %copy-start.3 = (bf16[3,16,128,320]{2,3,1,0:T(8,128)(2,1)}, bf16[3,16,128,320]{2,3,1,0:T(8,128)(2,1)S(1)}, u32[]{:S(2)}) copy-start(bf16[3,16,128,320]{2,3,1,0:T(8,128)(2,1)S(1)} %multiply_convert_fusion) | copy-start | bytes 11796484
  178.0 14.5 %slice-start.3 = ((s8[8847360]{0:T(1024)(128)(4,1)}), s8[4194304]{0:T(1024)(128)(4,1)S(1)}, s32[]{:S(2)}) async-start(s8[8847360]{0:T(1024)(128)(4,1)} %bitcast.301), calls=%async_computation.8 | async-start | bytes 8388608
  178.0 14.5 %slice-start.4 = ((s8[8847360]{0:T(1024)(128)(4,1)}), s8[4194304]{0:T(1024)(128)(4,1)S(1)}, s32[]{:S(2)}) async-start(s8[8847360]{0:T(1024)(128)(4,1)} %bitcast.301), calls=%async_computation.9 | async-start | bytes 8388608
  183.7 136.3 %collective-permute-start.2 = (bf16[3,1,128,320]{2,3,1,0:T(8,128)(2,1)S(1)}, bf16[3,1,128,320]{2,3,1,0:T(8,128)(2,1)S(1)}, u32[]{:S(2)}, u32[]{:S(2)}) collective-permute-start(bf16[3,1,128,320]{2,3,1,0:T(8,128)(2,1)S(1)} %get-tuple-element.16), channel_id=1, source_target_pairs={{0,2},{2,4},{4,6},{6,8},{8,10},{10,12},{12,14},{1,3},{3,5},{5,7},{... | collective-permute-start | bytes 737288 | tf_op jit(solution)/shard_map/ppermute | solution.py:16
  185.1 7.5 %slice-start.5 = ((s8[8847360]{0:T(1024)(128)(4,1)}), s8[458752]{0:T(1024)(128)(4,1)S(1)}, s32[]{:S(2)}) async-start(s8[8847360]{0:T(1024)(128)(4,1)} %bitcast.301), calls=%async_computation.10 | async-start | bytes 917504
  185.1 129.7 %collective-permute-start.3 = (bf16[3,1,128,320]{2,3,1,0:T(8,128)(2,1)S(1)}, bf16[3,1,128,320]{2,3,1,0:T(8,128)(2,1)S(1)}, u32[]{:S(2)}, u32[]{:S(2)}) collective-permute-start(bf16[3,1,128,320]{2,3,1,0:T(8,128)(2,1)S(1)} %get-tuple-element.17), channel_id=1, source_target_pairs={{2,0},{4,2},{6,4},{8,6},{10,8},{12,10},{14,12},{3,1},{5,3},{7,5},{... | collective-permute-start | bytes 737288 | tf_op jit(solution)/shard_map/ppermute | solution.py:18
  208.6 2.2 copy-start.10
  216.4 7.6 %copy-start.7 = (bf16[3,16,128,320]{2,3,1,0:T(8,128)(2,1)S(1)}, bf16[3,16,128,320]{2,3,1,0:T(8,128)(2,1)}, u32[]{:S(2)}) copy-start(bf16[3,16,128,320]{2,3,1,0:T(8,128)(2,1)} %get-tuple-element.20) | copy-start | bytes 11796484
  216.4 7.6 %copy-start.14 = (bf16[3,16,128,320]{2,3,1,0:T(8,128)(2,1)S(1)}, bf16[3,16,128,320]{2,3,1,0:T(8,128)(2,1)}, u32[]{:S(2)}) copy-start(bf16[3,16,128,320]{2,3,1,0:T(8,128)(2,1)} %param.17) | copy-start | bytes 11796484
  224.0 2.2 copy-start.8
  228.6 182.9 %all-reduce.5.cloned.1.call-start = ((), (), s32[]{:S(2)}) async-start(), calls=%async_computation.3 | async-start | bytes 1024000 | tf_op jit(solution)/shard_map/psum | solution.py:128
  228.7 9.0 %copy-start.11 = (bf16[320,3,3,320]{3,0,2,1:T(8,128)(2,1)S(1)}, bf16[320,3,3,320]{3,0,2,1:T(8,128)(2,1)}, u32[]{:S(2)}) copy-start(bf16[320,3,3,320]{3,0,2,1:T(8,128)(2,1)} %all-gather.4.cloned.1.call-done) | copy-start | bytes 5529604
  228.7 16.5 %slice-start = ((s8[8847360]{0:T(1024)(128)(4,1)}), s8[4194304]{0:T(1024)(128)(4,1)S(1)}, s32[]{:S(2)}) async-start(s8[8847360]{0:T(1024)(128)(4,1)} %bitcast.299), calls=%async_computation.5 | async-start | bytes 8388608
  228.7 16.5 %slice-start.1 = ((s8[8847360]{0:T(1024)(128)(4,1)}), s8[4194304]{0:T(1024)(128)(4,1)S(1)}, s32[]{:S(2)}) async-start(s8[8847360]{0:T(1024)(128)(4,1)} %bitcast.299), calls=%async_computation.6 | async-start | bytes 8388608
  237.7 7.5 %slice-start.2 = ((s8[8847360]{0:T(1024)(128)(4,1)}), s8[458752]{0:T(1024)(128)(4,1)S(1)}, s32[]{:S(2)}) async-start(s8[8847360]{0:T(1024)(128)(4,1)} %bitcast.299), calls=%async_computation.7 | async-start | bytes 917504
  307.2 7.6 %copy-start.4 = (bf16[3,16,128,320]{2,3,1,0:T(8,128)(2,1)S(1)}, bf16[3,16,128,320]{2,3,1,0:T(8,128)(2,1)}, u32[]{:S(2)}) copy-start(bf16[3,16,128,320]{2,3,1,0:T(8,128)(2,1)} %copy-done.3) | copy-start | bytes 11796484
  359.0 5.4 %copy-start.12 = (s32[3,16,128]{2,1,0:T(8,128)S(1)}, s32[3,16,128]{2,1,0:T(8,128)}, u32[]{:S(2)}) copy-start(s32[3,16,128]{2,1,0:T(8,128)} %param.10) | copy-start | bytes 73732
  364.4 51.0 %copy-start.1 = (bf16[1280,320]{0,1:T(8,128)(2,1)S(1)}, bf16[1280,320]{0,1:T(8,128)(2,1)}, u32[]{:S(2)}) copy-start(bf16[1280,320]{0,1:T(8,128)(2,1)} %param.13) | copy-start | bytes 2457604
Sparse Core Ops, SparseCore 0:
  10.2 66.9 all-gather.5
  79.4 49.2 all-gather.3
  228.7 87.1 reduce-scatter.3
  364.5 20.1 all-reduce.4
